TPU v7x, 128 devices: a whole 4x4x4 slice. The times are simulated.
128 devices in a mesh: patch: 32 (over x, z, core), grp: 4 (over y).
Axes of the slice: x: 4, y: 4, z: 4, core: 2. Of those that a mesh axis runs over, the one named last changes fastest.
Arguments:
- incident: float32 [16, 262144], P(None, ('patch', 'grp')), may hold values from -6 to 6
- self_term: float32 [262144], P(('patch', 'grp')), may hold values from 1 to 3
- near_field: bfloat16 [262144, 2304], P(('patch', 'grp')), may hold values from -0.125 to 0.125
- history: bfloat16 [8, 16, 262144], P(None, None, 'patch'), may hold values from -6 to 6
- ret_values: bfloat16 [32768, 128, 128], P(('patch', 'grp')), may hold values from -0.125 to 0.125
- slot_row: int32 [32768], P(('patch', 'grp')), may hold values from 0 to 15
- slot_col: int32 [32768], P(('patch', 'grp')), may hold values from 0 to 191
- slot_delay: int32 [32768], P(('patch', 'grp')), may hold values from 0 to 7
- live_count: int32 [128], P(('patch', 'grp')), may hold values from 32 to 256, as said below
Outputs:
- current: float32 [16, 262144], P(None, ('patch', 'grp'))
- newest: bfloat16 [16, 262144], P(None, 'patch')
Inputs may be any that keep to these rules, and one draw needn't show every extreme that they name: The first live_count[d] slots of shard d are live, the rest ignored; some shard has all 256 slots live.
All inputs are finite; a program needn't handle non-finite values.
Results may differ from a plain program's by a relative error of at most 0.0055.
Values may be sent and summed in bfloat16 or wider, within the bound.
No kernel may reach another device: no remote copies, remote signals or barrier semaphores. Data moves between devices by JAX's collectives and lax.ppermute only.
A program may use at most 128 MiB of HBM per device.

v0:
```python
import jax
import jax.numpy as jnp
from jax import lax
from jax.sharding import PartitionSpec as P

BLK = 128
DELAYS = 8
SWEEPS = 4
RB = 16
SLOTS = 256


def extended_2(block, sides, width):
    for axis, dim in sides:
        count = lax.axis_size(axis)
        forward = [(i, i + 1) for i in range(count - 1)]
        backward = [(target, source) for source, target in forward]
        low = lax.ppermute(
            lax.slice_in_dim(block, block.shape[dim] - width, None, axis=dim), axis, forward
        )
        high = lax.ppermute(lax.slice_in_dim(block, 0, width, axis=dim), axis, backward)
        block = jnp.concatenate([low, block, high], axis=dim)
    return block


def body(
    incident, self_term, near_field, history, ret_values, slot_row, slot_col, slot_delay, live_count
):
    waves = incident.shape[0]
    own_cols = incident.shape[1]
    group_idx = lax.axis_index("grp")
    window = extended_2(history, (("patch", 2),), history.shape[2])
    grouped = window.reshape(DELAYS, waves, window.shape[2] // BLK, BLK)
    limit = live_count[0]
    blocks = grouped[slot_delay, :, slot_col, :]
    prods = jnp.einsum("swj,sij->swi", blocks, ret_values, preferred_element_type=jnp.float32)
    alive = (jnp.arange(SLOTS, dtype=jnp.int32) < limit).astype(jnp.float32)
    onehot = (slot_row[None, :] == jnp.arange(RB, dtype=jnp.int32)[:, None]).astype(
        jnp.float32
    ) * alive[None, :]
    retarded = jnp.einsum("rs,swi->wri", onehot, prods, precision=lax.Precision.HIGHEST)
    rhs = incident - retarded.reshape(waves, own_cols)
    sweep_in = lax.dynamic_slice_in_dim(history[0], group_idx * own_cols, own_cols, 1)
    current = sweep_in.astype(jnp.float32)
    for sweep in range(SWEEPS):
        extended = extended_2(sweep_in, (("patch", 1),), BLK)
        coupling = lax.dot_general(
            extended, near_field, (((1,), (1,)), ((), ())), preferred_element_type=jnp.float32
        )
        current = (rhs - coupling) / self_term[None, :]
        sweep_in = current.astype(jnp.bfloat16)
    newest = lax.all_gather(sweep_in, "grp", axis=1, tiled=True)
    return (current, newest)


def solution(mesh):
    placed = (
        P(None, ("patch", "grp")),
        P(("patch", "grp")),
        P(("patch", "grp"), None),
        P(None, None, "patch"),
        P(("patch", "grp"), None, None),
        P(("patch", "grp")),
        P(("patch", "grp")),
        P(("patch", "grp")),
        P(("patch", "grp")),
    )
    return jax.shard_map(
        body,
        mesh=mesh,
        in_specs=placed,
        out_specs=(P(None, ("patch", "grp")), P(None, "patch")),
        check_vma=False,
    )
```

profile of v0, /device:TPU:6, one launch (start us, length us, event | category | flops | bytes accessed | tf_op | source)
XLA Modules:
  0.0 111.1 jit_solution(12761360910164445370)
XLA Ops:
  0.6 5.7 %collective-permute-start.1 = (bf16[8,16,8192]{2,1,0:T(8,128)(2,1)}, bf16[8,16,8192]{2,1,0:T(8,128)(2,1)S(1)}, u32[]{:S(2)}, u32[]{:S(2)}) collective-permute-start(bf16[8,16,8192]{2,1,0:T(8,128)(2,1)} %param.12), channel_id=1, source_target_pairs={{4,0},{8,4},{12,8},{16,12},{20,16},{24,20},{28,24},{32,28},{36,32}... | collective-permute-start | bytes 6291464 | tf_op jit(solution)/shard_map/ppermute | solution.py:21
  6.3 1.9 %collective-permute-start = (bf16[8,16,8192]{2,1,0:T(8,128)(2,1)}, bf16[8,16,8192]{2,1,0:T(8,128)(2,1)}, u32[]{:S(2)}, u32[]{:S(2)}) collective-permute-start(bf16[8,16,8192]{2,1,0:T(8,128)(2,1)} %param.12), channel_id=1, source_target_pairs={{0,4},{4,8},{8,12},{12,16},{16,20},{20,24},{24,28},{28,32},{32,36}... | collective-permute-start | bytes 6291464 | tf_op jit(solution)/shard_map/ppermute | solution.py:18
  8.2 1.0 slice.27
  9.2 5.8 %collective-permute-start.3 = (bf16[16,128]{1,0:T(8,128)(2,1)S(1)}, bf16[16,128]{1,0:T(8,128)(2,1)S(1)}, u32[]{:S(2)}, u32[]{:S(2)}) collective-permute-start(bf16[16,128]{1,0:T(8,128)(2,1)S(1)} %get-tuple-element.9), channel_id=1, source_target_pairs={{4,0},{8,4},{12,8},{16,12},{20,16},{24,20},{28,24},{32,28},{36,32}... | collective-permute-start | bytes 12296 | tf_op jit(solution)/shard_map/ppermute | solution.py:21
  15.0 1.9 %collective-permute-start.2 = (bf16[16,128]{1,0:T(8,128)(2,1)S(1)}, bf16[16,128]{1,0:T(8,128)(2,1)S(1)}, u32[]{:S(2)}, u32[]{:S(2)}) collective-permute-start(bf16[16,128]{1,0:T(8,128)(2,1)S(1)} %get-tuple-element.8), channel_id=1, source_target_pairs={{0,4},{4,8},{8,12},{12,16},{16,20},{20,24},{24,28},{28,32},{32,36}... | collective-permute-start | bytes 12296 | tf_op jit(solution)/shard_map/ppermute | solution.py:18
  17.6 0.7 fusion.36
  18.3 11.8 %collective-permute-done.1 = bf16[8,16,8192]{2,1,0:T(8,128)(2,1)S(1)} collective-permute-done((bf16[8,16,8192]{2,1,0:T(8,128)(2,1)}, bf16[8,16,8192]{2,1,0:T(8,128)(2,1)S(1)}, u32[]{:S(2)}, u32[]{:S(2)}) %collective-permute-start.1) | collective-permute-done | bytes 2097184 | tf_op jit(solution)/shard_map/ppermute | solution.py:21
  30.1 5.9 %collective-permute-done = bf16[8,16,8192]{2,1,0:T(8,128)(2,1)} collective-permute-done((bf16[8,16,8192]{2,1,0:T(8,128)(2,1)}, bf16[8,16,8192]{2,1,0:T(8,128)(2,1)}, u32[]{:S(2)}, u32[]{:S(2)}) %collective-permute-start) | collective-permute-done | bytes 2097184 | tf_op jit(solution)/shard_map/ppermute | solution.py:18
  36.1 7.2 %copy_bitcast_fusion = bf16[8,16,192,128]{3,1,2,0:T(8,128)(2,1)} fusion(bf16[8,16,8192]{2,1,0:T(8,128)(2,1)S(1)} %collective-permute-done.1, bf16[8,16,8192]{2,1,0:T(8,128)(2,1)} %param.12, bf16[8,16,8192]{2,1,0:T(8,128)(2,1)} %collective-permute-done), kind=kLoop, calls=%fused_computation.1 | loop fusion | flops 18874368 | bytes 12582912 | tf_op jit(solution)/shard_map/reshape | solution.py:33
  43.2 4.0 %gather_fusion = bf16[256,16,128]{2,1,0:T(8,128)(2,1)S(1)} fusion(bf16[8,16,192,128]{3,1,2,0:T(8,128)(2,1)} %copy_bitcast_fusion, s32[256]{0:T(256)S(1)} %fusion.36), kind=kCustom, calls=%fused_computation | custom fusion | bytes 2099200 | tf_op jit(solution)/shard_map/gather | solution.py:35
  47.2 0.0 copy-start.2
  47.3 0.0 slice-start
  47.3 6.9 %fusion.49 = f32[256,16,128]{2,1,0:T(8,128)S(1)} fusion(bf16[256,16,128]{2,1,0:T(8,128)(2,1)S(1)} %gather_fusion, bf16[256,128,128]{2,1,0:T(8,128)(2,1)} %param.13), kind=kOutput, calls=%fused_computation.62 | convolution fusion | flops 134217728 | bytes 11534336 | tf_op jit(solution)/shard_map/swj,sij->swi/dot_general | solution.py:36
  54.2 1.8 %fusion.7 = f32[16,128,16]{1,2,0:T(8,128)S(1)} fusion(f32[256,16,128]{2,1,0:T(8,128)S(1)} %fusion.49, f32[256]{0:T(256)S(1)} %compare_convert_fusion, s32[256]{0:T(256)S(1)} %copy-done.2), kind=kOutput, calls=%fused_computation.14 | convolution fusion | flops 100671488 | bytes 2230272 | tf_op jit(solution)/shard_map/rs,swi->wri/dot_general | solution.py:41
  56.0 0.0 copy-done.1
  56.0 0.1 bitcast_subtract_fusion
  56.0 0.0 slice-start.2
  56.1 6.3 %fusion.4 = bf16[16,2048]{1,0:T(8,128)(2,1)S(1)} fusion(f32[16,2048]{1,0:T(8,128)S(1)} %bitcast_subtract_fusion, bf16[2048,2304]{1,0:T(8,128)(2,1)} %param.11, bf16[16,128]{1,0:T(8,128)(2,1)S(1)} %collective-permute-done.3, bf16[16,2048]{1,0:T(8,128)(2,1)S(1)} %dynamic-slice_bitcast_fusion, bf16[16,128]{1,0:T(8,128)(2,1)S(1)} %collective-permute-done.2, ...), kind=kOutput, calls=%fused_computation.11 | convolution fusion | flops 151314432 | bytes 9715712 | tf_op jit(solution)/shard_map/dot_general | solution.py:47
  62.4 1.9 %collective-permute-start.5 = (bf16[16,128]{1,0:T(8,128)(2,1)S(1)}, bf16[16,128]{1,0:T(8,128)(2,1)S(1)}, u32[]{:S(2)}, u32[]{:S(2)}) collective-permute-start(bf16[16,128]{1,0:T(8,128)(2,1)S(1)} %get-tuple-element.7), channel_id=1, source_target_pairs={{4,0},{8,4},{12,8},{16,12},{20,16},{24,20},{28,24},{32,28},{36,32}... | collective-permute-start | bytes 12296 | tf_op jit(solution)/shard_map/ppermute | solution.py:21
  64.3 2.4 %collective-permute-start.4 = (bf16[16,128]{1,0:T(8,128)(2,1)S(1)}, bf16[16,128]{1,0:T(8,128)(2,1)S(1)}, u32[]{:S(2)}, u32[]{:S(2)}) collective-permute-start(bf16[16,128]{1,0:T(8,128)(2,1)S(1)} %get-tuple-element.6), channel_id=1, source_target_pairs={{0,4},{4,8},{8,12},{12,16},{16,20},{20,24},{24,28},{28,32},{32,36}... | collective-permute-start | bytes 12296 | tf_op jit(solution)/shard_map/ppermute | solution.py:18
  66.8 4.6 %collective-permute-done.4 = bf16[16,128]{1,0:T(8,128)(2,1)S(1)} collective-permute-done((bf16[16,128]{1,0:T(8,128)(2,1)S(1)}, bf16[16,128]{1,0:T(8,128)(2,1)S(1)}, u32[]{:S(2)}, u32[]{:S(2)}) %collective-permute-start.4) | collective-permute-done | bytes 4128 | tf_op jit(solution)/shard_map/ppermute | solution.py:18
  71.4 2.5 %fusion.5 = bf16[16,2048]{1,0:T(8,128)(2,1)S(1)} fusion(f32[16,2048]{1,0:T(8,128)S(1)} %bitcast_subtract_fusion, bf16[2048,2304]{1,0:T(8,128)(2,1)S(1)} %bitcast.23, bf16[16,128]{1,0:T(8,128)(2,1)S(1)} %collective-permute-done.5, bf16[16,2048]{1,0:T(8,128)(2,1)S(1)} %fusion.4, bf16[16,128]{1,0:T(8,128)(2,1)S(1)} %collective-permute-done.4, f32[2048]{0:T(1024)S(1)} %copy-done), kind=kOutput, calls=%fused_computation.12 | convolution fusion | flops 151314432 | bytes 9715712 | tf_op jit(solution)/shard_map/dot_general | solution.py:47
  73.9 1.9 %collective-permute-start.7 = (bf16[16,128]{1,0:T(8,128)(2,1)S(1)}, bf16[16,128]{1,0:T(8,128)(2,1)S(1)}, u32[]{:S(2)}, u32[]{:S(2)}) collective-permute-start(bf16[16,128]{1,0:T(8,128)(2,1)S(1)} %get-tuple-element.5), channel_id=1, source_target_pairs={{4,0},{8,4},{12,8},{16,12},{20,16},{24,20},{28,24},{32,28},{36,32}... | collective-permute-start | bytes 12296 | tf_op jit(solution)/shard_map/ppermute | solution.py:21
  75.9 2.4 %collective-permute-start.6 = (bf16[16,128]{1,0:T(8,128)(2,1)S(1)}, bf16[16,128]{1,0:T(8,128)(2,1)S(1)}, u32[]{:S(2)}, u32[]{:S(2)}) collective-permute-start(bf16[16,128]{1,0:T(8,128)(2,1)S(1)} %get-tuple-element.4), channel_id=1, source_target_pairs={{0,4},{4,8},{8,12},{12,16},{16,20},{20,24},{24,28},{28,32},{32,36}... | collective-permute-start | bytes 12296 | tf_op jit(solution)/shard_map/ppermute | solution.py:18
  78.3 4.6 %collective-permute-done.6 = bf16[16,128]{1,0:T(8,128)(2,1)S(1)} collective-permute-done((bf16[16,128]{1,0:T(8,128)(2,1)S(1)}, bf16[16,128]{1,0:T(8,128)(2,1)S(1)}, u32[]{:S(2)}, u32[]{:S(2)}) %collective-permute-start.6) | collective-permute-done | bytes 4128 | tf_op jit(solution)/shard_map/ppermute | solution.py:18
  82.9 2.5 %fusion.6 = bf16[16,2048]{1,0:T(8,128)(2,1)S(1)} fusion(f32[16,2048]{1,0:T(8,128)S(1)} %bitcast_subtract_fusion, bf16[2048,2304]{1,0:T(8,128)(2,1)S(1)} %bitcast.23, bf16[16,128]{1,0:T(8,128)(2,1)S(1)} %collective-permute-done.7, bf16[16,2048]{1,0:T(8,128)(2,1)S(1)} %fusion.5, bf16[16,128]{1,0:T(8,128)(2,1)S(1)} %collective-permute-done.6, f32[2048]{0:T(1024)S(1)} %copy-done), kind=kOutput, calls=%fused_computation.13 | convolution fusion | flops 151314432 | bytes 9715712 | tf_op jit(solution)/shard_map/dot_general | solution.py:47
  85.5 1.9 %collective-permute-start.9 = (bf16[16,128]{1,0:T(8,128)(2,1)S(1)}, bf16[16,128]{1,0:T(8,128)(2,1)S(1)}, u32[]{:S(2)}, u32[]{:S(2)}) collective-permute-start(bf16[16,128]{1,0:T(8,128)(2,1)S(1)} %get-tuple-element.3), channel_id=1, source_target_pairs={{4,0},{8,4},{12,8},{16,12},{20,16},{24,20},{28,24},{32,28},{36,32}... | collective-permute-start | bytes 12296 | tf_op jit(solution)/shard_map/ppermute | solution.py:21
  87.4 2.4 %collective-permute-start.8 = (bf16[16,128]{1,0:T(8,128)(2,1)S(1)}, bf16[16,128]{1,0:T(8,128)(2,1)S(1)}, u32[]{:S(2)}, u32[]{:S(2)}) collective-permute-start(bf16[16,128]{1,0:T(8,128)(2,1)S(1)} %get-tuple-element.2), channel_id=1, source_target_pairs={{0,4},{4,8},{8,12},{12,16},{16,20},{20,24},{24,28},{28,32},{32,36}... | collective-permute-start | bytes 12296 | tf_op jit(solution)/shard_map/ppermute | solution.py:18
  89.8 4.6 %collective-permute-done.8 = bf16[16,128]{1,0:T(8,128)(2,1)S(1)} collective-permute-done((bf16[16,128]{1,0:T(8,128)(2,1)S(1)}, bf16[16,128]{1,0:T(8,128)(2,1)S(1)}, u32[]{:S(2)}, u32[]{:S(2)}) %collective-permute-start.8) | collective-permute-done | bytes 4128 | tf_op jit(solution)/shard_map/ppermute | solution.py:18
  94.4 3.2 %fusion.48 = (bf16[16,2048]{1,0:T(8,128)(2,1)S(1)}, f32[16,2048]{1,0:T(8,128)}) fusion(f32[2048]{0:T(1024)S(1)} %copy-done, f32[16,2048]{1,0:T(8,128)S(1)} %bitcast_subtract_fusion, bf16[2048,2304]{1,0:T(8,128)(2,1)S(1)} %bitcast.23, bf16[16,128]{1,0:T(8,128)(2,1)S(1)} %collective-permute-done.9, bf16[16,2048]{1,0:T(8,128)(2,1)S(1)} %fusion.6, ...), kind=kOutput, calls=%fused_computation.61 | convolution fusion | flops 151314432 | bytes 9846784 | tf_op jit(solution)/shard_map/dot_general | solution.py:47
  97.6 12.8 %all_gather.3 = bf16[16,8192]{1,0:T(8,128)(2,1)S(1)} all-gather(bf16[16,2048]{1,0:T(8,128)(2,1)S(1)} %get-tuple-element.10), channel_id=1, replica_groups=mesh['patch'=32,'grp'=4] {'grp'}, dimensions={1}, use_global_device_ids=true | all-gather | bytes 327680 | tf_op jit(solution)/shard_map/all_gather | solution.py:52
  110.4 0.7 copy.21
  (20 shorter events, 0.1 us)
Async XLA Ops:
  0.6 29.5 %collective-permute-start.1 = (bf16[8,16,8192]{2,1,0:T(8,128)(2,1)}, bf16[8,16,8192]{2,1,0:T(8,128)(2,1)S(1)}, u32[]{:S(2)}, u32[]{:S(2)}) collective-permute-start(bf16[8,16,8192]{2,1,0:T(8,128)(2,1)} %param.12), channel_id=1, source_target_pairs={{4,0},{8,4},{12,8},{16,12},{20,16},{24,20},{28,24},{32,28},{36,32}... | collective-permute-start | bytes 6291464 | tf_op jit(solution)/shard_map/ppermute | solution.py:21
  6.3 29.8 %collective-permute-start = (bf16[8,16,8192]{2,1,0:T(8,128)(2,1)}, bf16[8,16,8192]{2,1,0:T(8,128)(2,1)}, u32[]{:S(2)}, u32[]{:S(2)}) collective-permute-start(bf16[8,16,8192]{2,1,0:T(8,128)(2,1)} %param.12), channel_id=1, source_target_pairs={{0,4},{4,8},{8,12},{12,16},{16,20},{20,24},{24,28},{28,32},{32,36}... | collective-permute-start | bytes 6291464 | tf_op jit(solution)/shard_map/ppermute | solution.py:18
  9.2 46.8 %collective-permute-start.3 = (bf16[16,128]{1,0:T(8,128)(2,1)S(1)}, bf16[16,128]{1,0:T(8,128)(2,1)S(1)}, u32[]{:S(2)}, u32[]{:S(2)}) collective-permute-start(bf16[16,128]{1,0:T(8,128)(2,1)S(1)} %get-tuple-element.9), channel_id=1, source_target_pairs={{4,0},{8,4},{12,8},{16,12},{20,16},{24,20},{28,24},{32,28},{36,32}... | collective-permute-start | bytes 12296 | tf_op jit(solution)/shard_map/ppermute | solution.py:21
  15.0 41.1 %collective-permute-start.2 = (bf16[16,128]{1,0:T(8,128)(2,1)S(1)}, bf16[16,128]{1,0:T(8,128)(2,1)S(1)}, u32[]{:S(2)}, u32[]{:S(2)}) collective-permute-start(bf16[16,128]{1,0:T(8,128)(2,1)S(1)} %get-tuple-element.8), channel_id=1, source_target_pairs={{0,4},{4,8},{8,12},{12,16},{16,20},{20,24},{24,28},{28,32},{32,36}... | collective-permute-start | bytes 12296 | tf_op jit(solution)/shard_map/ppermute | solution.py:18
  47.2 7.0 %copy-start.2 = (s32[256]{0:T(256)S(1)}, s32[256]{0:T(256)}, u32[]{:S(2)}) copy-start(s32[256]{0:T(256)} %param.14) | copy-start | bytes 3076
  47.3 8.7 %copy-start.1 = (f32[16,2048]{1,0:T(8,128)S(1)}, f32[16,2048]{1,0:T(8,128)}, u32[]{:S(2)}) copy-start(f32[16,2048]{1,0:T(8,128)} %param.9) | copy-start | bytes 393220
  47.3 8.8 %copy-start = (f32[2048]{0:T(1024)S(1)}, f32[2048]{0:T(1024)}, u32[]{:S(2)}) copy-start(f32[2048]{0:T(1024)} %param.10) | copy-start | bytes 24580
  47.3 24.1 %slice-start = ((s8[9437184]{0:T(1024)(128)(4,1)}), s8[4194304]{0:T(1024)(128)(4,1)S(1)}, s32[]{:S(2)}) async-start(s8[9437184]{0:T(1024)(128)(4,1)} %bitcast.22), calls=%async_computation | async-start | bytes 8388608
  47.3 24.1 %slice-start.1 = ((s8[9437184]{0:T(1024)(128)(4,1)}), s8[4194304]{0:T(1024)(128)(4,1)S(1)}, s32[]{:S(2)}) async-start(s8[9437184]{0:T(1024)(128)(4,1)} %bitcast.22), calls=%async_computation.1 | async-start | bytes 8388608
  56.0 15.3 %slice-start.2 = ((s8[9437184]{0:T(1024)(128)(4,1)}), s8[1048576]{0:T(1024)(128)(4,1)S(1)}, s32[]{:S(2)}) async-start(s8[9437184]{0:T(1024)(128)(4,1)} %bitcast.22), calls=%async_computation.2 | async-start | bytes 2097152
  62.4 4.3 %collective-permute-start.5 = (bf16[16,128]{1,0:T(8,128)(2,1)S(1)}, bf16[16,128]{1,0:T(8,128)(2,1)S(1)}, u32[]{:S(2)}, u32[]{:S(2)}) collective-permute-start(bf16[16,128]{1,0:T(8,128)(2,1)S(1)} %get-tuple-element.7), channel_id=1, source_target_pairs={{4,0},{8,4},{12,8},{16,12},{20,16},{24,20},{28,24},{32,28},{36,32}... | collective-permute-start | bytes 12296 | tf_op jit(solution)/shard_map/ppermute | solution.py:21
  64.3 7.0 %collective-permute-start.4 = (bf16[16,128]{1,0:T(8,128)(2,1)S(1)}, bf16[16,128]{1,0:T(8,128)(2,1)S(1)}, u32[]{:S(2)}, u32[]{:S(2)}) collective-permute-start(bf16[16,128]{1,0:T(8,128)(2,1)S(1)} %get-tuple-element.6), channel_id=1, source_target_pairs={{0,4},{4,8},{8,12},{12,16},{16,20},{20,24},{24,28},{28,32},{32,36}... | collective-permute-start | bytes 12296 | tf_op jit(solution)/shard_map/ppermute | solution.py:18
  73.9 4.3 %collective-permute-start.7 = (bf16[16,128]{1,0:T(8,128)(2,1)S(1)}, bf16[16,128]{1,0:T(8,128)(2,1)S(1)}, u32[]{:S(2)}, u32[]{:S(2)}) collective-permute-start(bf16[16,128]{1,0:T(8,128)(2,1)S(1)} %get-tuple-element.5), channel_id=1, source_target_pairs={{4,0},{8,4},{12,8},{16,12},{20,16},{24,20},{28,24},{32,28},{36,32}... | collective-permute-start | bytes 12296 | tf_op jit(solution)/shard_map/ppermute | solution.py:21
  75.9 7.0 %collective-permute-start.6 = (bf16[16,128]{1,0:T(8,128)(2,1)S(1)}, bf16[16,128]{1,0:T(8,128)(2,1)S(1)}, u32[]{:S(2)}, u32[]{:S(2)}) collective-permute-start(bf16[16,128]{1,0:T(8,128)(2,1)S(1)} %get-tuple-element.4), channel_id=1, source_target_pairs={{0,4},{4,8},{8,12},{12,16},{16,20},{20,24},{24,28},{28,32},{32,36}... | collective-permute-start | bytes 12296 | tf_op jit(solution)/shard_map/ppermute | solution.py:18
  85.5 4.3 %collective-permute-start.9 = (bf16[16,128]{1,0:T(8,128)(2,1)S(1)}, bf16[16,128]{1,0:T(8,128)(2,1)S(1)}, u32[]{:S(2)}, u32[]{:S(2)}) collective-permute-start(bf16[16,128]{1,0:T(8,128)(2,1)S(1)} %get-tuple-element.3), channel_id=1, source_target_pairs={{4,0},{8,4},{12,8},{16,12},{20,16},{24,20},{28,24},{32,28},{36,32}... | collective-permute-start | bytes 12296 | tf_op jit(solution)/shard_map/ppermute | solution.py:21
  87.4 7.0 %collective-permute-start.8 = (bf16[16,128]{1,0:T(8,128)(2,1)S(1)}, bf16[16,128]{1,0:T(8,128)(2,1)S(1)}, u32[]{:S(2)}, u32[]{:S(2)}) collective-permute-start(bf16[16,128]{1,0:T(8,128)(2,1)S(1)} %get-tuple-element.2), channel_id=1, source_target_pairs={{0,4},{4,8},{8,12},{12,16},{16,20},{20,24},{24,28},{28,32},{32,36}... | collective-permute-start | bytes 12296 | tf_op jit(solution)/shard_map/ppermute | solution.py:18
where the time goes:
time: 112 us; the launch traced here: 111 us
  waiting for transfers between devices  31.6 us (28%)
  starting transfers between devices  28.2 us (25%)
  matrix products  23.2 us (21%)
  blocking collectives  12.8 us (11%)
  other arithmetic  7.93 us (7%)
  local copies, waits for them, and re-layouts  5.77 us (5%)
  between operations  1.54 us (1%)
    ppermute x5, waiting for transfers between devices, extended_2(): lax.ppermute(lax.slice_in_dim(block, block.shape[dim] - width, None, axis...  19.8 us
    ppermute x5, starting transfers between devices, extended_2(): lax.ppermute(lax.slice_in_dim(block, 0, width, axis=dim), axis, backward)  17.2 us
    dot_general x4, matrix products, body(): lax.dot_general(extended, near_field, (((1,), (1,)), ((), ())), preferred...  14.6 us
    all_gather x1, blocking collectives, body(): newest = lax.all_gather(sweep_in, 'grp', axis=1, tiled=True)  12.8 us
    ppermute x5, waiting for transfers between devices, extended_2(): lax.ppermute(lax.slice_in_dim(block, 0, width, axis=dim), axis, backward)  11.9 us
    ppermute x5, starting transfers between devices, extended_2(): lax.ppermute(lax.slice_in_dim(block, block.shape[dim] - width, None, axis...  11.1 us
    reshape x1, other arithmetic, body(): grouped = window.reshape(DELAYS, waves, window.shape[2] // BLK, BLK)  7.16 us
    dot_general x1, matrix products, body(): jnp.einsum('swj,sij->swi', blocks, ret_values, preferred_element_type=jnp...  6.91 us
  transfers between devices with their start and end apart: 10, of which 5 were waited for; matrix products, arithmetic and copies ran while one was open for 19% of the time, Pallas kernels for 0%

commit v1 on v0

--- a/solution.py
+++ b/solution.py
@@ -49,7 +49,21 @@
         )
         current = (rhs - coupling) / self_term[None, :]
         sweep_in = current.astype(jnp.bfloat16)
-    newest = lax.all_gather(sweep_in, "grp", axis=1, tiled=True)
+    ways, here, turn = (lax.axis_size("grp"), lax.axis_index("grp"), sweep_in.shape[1])
+    lengths = [n * ways if d == 1 else n for d, n in enumerate(sweep_in.shape)]
+    full = lax.dynamic_update_slice_in_dim(
+        jnp.zeros(lengths, sweep_in.dtype), sweep_in, here * turn, axis=1
+    )
+    going_up = going_down = sweep_in
+    for far in range(1, ways // 2 + 1):
+        going_up = lax.ppermute(going_up, "grp", [(d, (d + 1) % ways) for d in range(ways)])
+        full = lax.dynamic_update_slice_in_dim(full, going_up, (here - far) % ways * turn, axis=1)
+        if 2 * far < ways:
+            going_down = lax.ppermute(going_down, "grp", [(d, (d - 1) % ways) for d in range(ways)])
+            full = lax.dynamic_update_slice_in_dim(
+                full, going_down, (here + far) % ways * turn, axis=1
+            )
+    newest = full
     return (current, newest)
 
 

time: 112 us -> 105 us (0.938)
  starting transfers between devices: 28.2 us -> 41.9 us
  blocking collectives: 12.8 us -> 0 us
  waiting for transfers between devices: 31.6 us -> 25.5 us
  other arithmetic: 7.93 us -> 6.43 us
    all_gather x1 -> x0, blocking collectives: 12.8 us -> none  [body(): newest = lax.all_gather(sweep_in, 'grp', axis=1, tiled=True)]
    ppermute x5, starting transfers between devices: 17.2 us -> 28.9 us  [extended_2(): lax.ppermute(lax.slice_in_dim(block, 0, width, axis=dim), axis, backward)]
    ppermute x0 -> x3, waiting for transfers between devices: none -> 7.87 us  [the longest x2 7.87 us: body(): lax.ppermute(going_up, 'grp', [(d, (d + 1) % ways) for d in range(ways)])]
    ppermute x5, waiting for transfers between devices: 19.8 us -> 11.9 us  [extended_2(): lax.ppermute(lax.slice_in_dim(block, block.shape[dim] - width, None, axis...]
    ppermute x5, waiting for transfers between devices: 11.9 us -> 5.75 us  [extended_2(): lax.ppermute(lax.slice_in_dim(block, 0, width, axis=dim), axis, backward)]
    ppermute x0 -> x3, starting transfers between devices: none -> 3.32 us  [the longest x2 1.66 us: body(): lax.ppermute(going_up, 'grp', [(d, (d + 1) % ways) for d in range(ways)])]
    reshape x1, other arithmetic: 7.16 us -> 5.67 us  [body(): grouped = window.reshape(DELAYS, waves, window.shape[2] // BLK, BLK)]
    ppermute x5, starting transfers between devices: 11.1 us -> 9.68 us  [extended_2(): lax.ppermute(lax.slice_in_dim(block, block.shape[dim] - width, None, axis...]
  transfers between devices with their start and end apart: 10 -> 13, of which waited for: 5 -> 7; matrix products, arithmetic and copies ran while one was open for 19% -> 19% of each run, Pallas kernels for 0% -> 0%
where the time goes in v1:
time: 105 us; the launch traced here: 104 us
  starting transfers between devices  41.9 us (40%)
  waiting for transfers between devices  25.5 us (24%)
  matrix products  23.2 us (22%)
  other arithmetic  6.43 us (6%)
  local copies, waits for them, and re-layouts  5.82 us (6%)
  between operations  1.57 us (1%)
    ppermute x5, starting transfers between devices, extended_2(): lax.ppermute(lax.slice_in_dim(block, 0, width, axis=dim), axis, backward)  28.9 us
    dot_general x4, matrix products, body(): lax.dot_general(extended, near_field, (((1,), (1,)), ((), ())), preferred...  14.6 us
    ppermute x5, waiting for transfers between devices, extended_2(): lax.ppermute(lax.slice_in_dim(block, block.shape[dim] - width, None, axis...  11.9 us
    ppermute x5, starting transfers between devices, extended_2(): lax.ppermute(lax.slice_in_dim(block, block.shape[dim] - width, None, axis...  9.68 us
    ppermute x2, waiting for transfers between devices, body(): lax.ppermute(going_up, 'grp', [(d, (d + 1) % ways) for d in range(ways)])  7.87 us
    dot_general x1, matrix products, body(): jnp.einsum('swj,sij->swi', blocks, ret_values, preferred_element_type=jnp...  6.91 us
    ppermute x5, waiting for transfers between devices, extended_2(): lax.ppermute(lax.slice_in_dim(block, 0, width, axis=dim), axis, backward)  5.75 us
    reshape x1, other arithmetic, body(): grouped = window.reshape(DELAYS, waves, window.shape[2] // BLK, BLK)  5.67 us
  transfers between devices with their start and end apart: 13, of which 7 were waited for; matrix products, arithmetic and copies ran while one was open for 19% of the time, Pallas kernels for 0%

profile of v1, /device:TPU:6, one launch (start us, length us, event | category | flops | bytes accessed | tf_op | source)
XLA Modules:
  0.0 104.5 jit_solution(6769765879820422670)
XLA Ops:
  0.6 1.9 %collective-permute-start = (bf16[8,16,8192]{2,1,0:T(8,128)(2,1)}, bf16[8,16,8192]{2,1,0:T(8,128)(2,1)S(1)}, u32[]{:S(2)}, u32[]{:S(2)}) collective-permute-start(bf16[8,16,8192]{2,1,0:T(8,128)(2,1)} %param.12), channel_id=1, source_target_pairs={{0,4},{4,8},{8,12},{12,16},{16,20},{20,24},{24,28},{28,32},{32,36}... | collective-permute-start | bytes 6291464 | tf_op jit(solution)/shard_map/ppermute | solution.py:18
  2.6 5.8 %collective-permute-start.1 = (bf16[8,16,8192]{2,1,0:T(8,128)(2,1)}, bf16[8,16,8192]{2,1,0:T(8,128)(2,1)}, u32[]{:S(2)}, u32[]{:S(2)}) collective-permute-start(bf16[8,16,8192]{2,1,0:T(8,128)(2,1)} %param.12), channel_id=1, source_target_pairs={{4,0},{8,4},{12,8},{16,12},{20,16},{24,20},{28,24},{32,28},{36,32}... | collective-permute-start | bytes 6291464 | tf_op jit(solution)/shard_map/ppermute | solution.py:21
  8.3 1.0 slice.27
  9.3 1.9 %collective-permute-start.2 = (bf16[16,128]{1,0:T(8,128)(2,1)S(1)}, bf16[16,128]{1,0:T(8,128)(2,1)S(1)}, u32[]{:S(2)}, u32[]{:S(2)}) collective-permute-start(bf16[16,128]{1,0:T(8,128)(2,1)S(1)} %get-tuple-element.10), channel_id=1, source_target_pairs={{0,4},{4,8},{8,12},{12,16},{16,20},{20,24},{24,28},{28,32},{32,36}... | collective-permute-start | bytes 12296 | tf_op jit(solution)/shard_map/ppermute | solution.py:18
  11.3 5.8 %collective-permute-start.3 = (bf16[16,128]{1,0:T(8,128)(2,1)S(1)}, bf16[16,128]{1,0:T(8,128)(2,1)S(1)}, u32[]{:S(2)}, u32[]{:S(2)}) collective-permute-start(bf16[16,128]{1,0:T(8,128)(2,1)S(1)} %get-tuple-element.11), channel_id=1, source_target_pairs={{4,0},{8,4},{12,8},{16,12},{20,16},{24,20},{28,24},{32,28},{36,32}... | collective-permute-start | bytes 12296 | tf_op jit(solution)/shard_map/ppermute | solution.py:21
  17.7 0.7 fusion.36
  18.4 11.9 %collective-permute-done = bf16[8,16,8192]{2,1,0:T(8,128)(2,1)S(1)} collective-permute-done((bf16[8,16,8192]{2,1,0:T(8,128)(2,1)}, bf16[8,16,8192]{2,1,0:T(8,128)(2,1)S(1)}, u32[]{:S(2)}, u32[]{:S(2)}) %collective-permute-start) | collective-permute-done | bytes 2097184 | tf_op jit(solution)/shard_map/ppermute | solution.py:18
  30.3 1.9 %collective-permute-done.1 = bf16[8,16,8192]{2,1,0:T(8,128)(2,1)} collective-permute-done((bf16[8,16,8192]{2,1,0:T(8,128)(2,1)}, bf16[8,16,8192]{2,1,0:T(8,128)(2,1)}, u32[]{:S(2)}, u32[]{:S(2)}) %collective-permute-start.1) | collective-permute-done | bytes 2097184 | tf_op jit(solution)/shard_map/ppermute | solution.py:21
  32.2 5.7 %copy_bitcast_fusion = bf16[8,16,192,128]{3,1,2,0:T(8,128)(2,1)} fusion(bf16[8,16,8192]{2,1,0:T(8,128)(2,1)} %collective-permute-done.1, bf16[8,16,8192]{2,1,0:T(8,128)(2,1)} %param.12, bf16[8,16,8192]{2,1,0:T(8,128)(2,1)S(1)} %collective-permute-done), kind=kLoop, calls=%fused_computation.1 | loop fusion | flops 18874368 | bytes 12582912 | tf_op jit(solution)/shard_map/reshape | solution.py:33
  37.8 4.0 %gather_fusion = bf16[256,16,128]{2,1,0:T(8,128)(2,1)S(1)} fusion(bf16[8,16,192,128]{3,1,2,0:T(8,128)(2,1)} %copy_bitcast_fusion, s32[256]{0:T(256)S(1)} %fusion.36), kind=kCustom, calls=%fused_computation | custom fusion | bytes 2099200 | tf_op jit(solution)/shard_map/gather | solution.py:35
  41.9 6.9 %fusion.48 = f32[256,16,128]{2,1,0:T(8,128)S(1)} fusion(bf16[256,16,128]{2,1,0:T(8,128)(2,1)S(1)} %gather_fusion, bf16[256,128,128]{2,1,0:T(8,128)(2,1)} %param.13), kind=kOutput, calls=%fused_computation.65 | convolution fusion | flops 134217728 | bytes 11534336 | tf_op jit(solution)/shard_map/swj,sij->swi/dot_general | solution.py:36
  48.8 1.8 %fusion.7 = f32[16,128,16]{1,2,0:T(8,128)S(1)} fusion(f32[256,16,128]{2,1,0:T(8,128)S(1)} %fusion.48, f32[256]{0:T(256)S(1)} %compare_convert_fusion, s32[256]{0:T(256)S(1)} %copy-done.3), kind=kOutput, calls=%fused_computation.14 | convolution fusion | flops 100671488 | bytes 2230272 | tf_op jit(solution)/shard_map/rs,swi->wri/dot_general | solution.py:41
  50.6 0.1 bitcast_subtract_fusion
  50.7 6.3 %fusion.4 = bf16[16,2048]{1,0:T(8,128)(2,1)S(1)} fusion(f32[16,2048]{1,0:T(8,128)S(1)} %bitcast_subtract_fusion, bf16[2048,2304]{1,0:T(8,128)(2,1)} %param.11, bf16[16,128]{1,0:T(8,128)(2,1)S(1)} %collective-permute-done.3, bf16[16,2048]{1,0:T(8,128)(2,1)S(1)} %dynamic-slice_bitcast_fusion, bf16[16,128]{1,0:T(8,128)(2,1)S(1)} %collective-permute-done.2, ...), kind=kOutput, calls=%fused_computation.11 | convolution fusion | flops 151314432 | bytes 9715712 | tf_op jit(solution)/shard_map/dot_general | solution.py:47
  57.0 2.0 %collective-permute-start.4 = (bf16[16,128]{1,0:T(8,128)(2,1)S(1)}, bf16[16,128]{1,0:T(8,128)(2,1)S(1)}, u32[]{:S(2)}, u32[]{:S(2)}) collective-permute-start(bf16[16,128]{1,0:T(8,128)(2,1)S(1)} %get-tuple-element.8), channel_id=1, source_target_pairs={{0,4},{4,8},{8,12},{12,16},{16,20},{20,24},{24,28},{28,32},{32,36}... | collective-permute-start | bytes 12296 | tf_op jit(solution)/shard_map/ppermute | solution.py:18
  59.0 5.9 %collective-permute-start.5 = (bf16[16,128]{1,0:T(8,128)(2,1)S(1)}, bf16[16,128]{1,0:T(8,128)(2,1)S(1)}, u32[]{:S(2)}, u32[]{:S(2)}) collective-permute-start(bf16[16,128]{1,0:T(8,128)(2,1)S(1)} %get-tuple-element.9), channel_id=1, source_target_pairs={{4,0},{8,4},{12,8},{16,12},{20,16},{24,20},{28,24},{32,28},{36,32}... | collective-permute-start | bytes 12296 | tf_op jit(solution)/shard_map/ppermute | solution.py:21
  64.9 1.3 %collective-permute-done.5 = bf16[16,128]{1,0:T(8,128)(2,1)S(1)} collective-permute-done((bf16[16,128]{1,0:T(8,128)(2,1)S(1)}, bf16[16,128]{1,0:T(8,128)(2,1)S(1)}, u32[]{:S(2)}, u32[]{:S(2)}) %collective-permute-start.5) | collective-permute-done | bytes 4128 | tf_op jit(solution)/shard_map/ppermute | solution.py:21
  66.2 2.5 %fusion.5 = bf16[16,2048]{1,0:T(8,128)(2,1)S(1)} fusion(f32[16,2048]{1,0:T(8,128)S(1)} %bitcast_subtract_fusion, bf16[2048,2304]{1,0:T(8,128)(2,1)S(1)} %bitcast.23, bf16[16,128]{1,0:T(8,128)(2,1)S(1)} %collective-permute-done.5, bf16[16,2048]{1,0:T(8,128)(2,1)S(1)} %fusion.4, bf16[16,128]{1,0:T(8,128)(2,1)S(1)} %collective-permute-done.4, ...), kind=kOutput, calls=%fused_computation.12 | convolution fusion | flops 151314432 | bytes 9715712 | tf_op jit(solution)/shard_map/dot_general | solution.py:47
  68.7 1.9 %collective-permute-start.6 = (bf16[16,128]{1,0:T(8,128)(2,1)S(1)}, bf16[16,128]{1,0:T(8,128)(2,1)S(1)}, u32[]{:S(2)}, u32[]{:S(2)}) collective-permute-start(bf16[16,128]{1,0:T(8,128)(2,1)S(1)} %get-tuple-element.6), channel_id=1, source_target_pairs={{0,4},{4,8},{8,12},{12,16},{16,20},{20,24},{24,28},{28,32},{32,36}... | collective-permute-start | bytes 12296 | tf_op jit(solution)/shard_map/ppermute | solution.py:18
  70.7 5.8 %collective-permute-start.7 = (bf16[16,128]{1,0:T(8,128)(2,1)S(1)}, bf16[16,128]{1,0:T(8,128)(2,1)S(1)}, u32[]{:S(2)}, u32[]{:S(2)}) collective-permute-start(bf16[16,128]{1,0:T(8,128)(2,1)S(1)} %get-tuple-element.7), channel_id=1, source_target_pairs={{4,0},{8,4},{12,8},{16,12},{20,16},{24,20},{28,24},{32,28},{36,32}... | collective-permute-start | bytes 12296 | tf_op jit(solution)/shard_map/ppermute | solution.py:21
  76.4 1.3 %collective-permute-done.7 = bf16[16,128]{1,0:T(8,128)(2,1)S(1)} collective-permute-done((bf16[16,128]{1,0:T(8,128)(2,1)S(1)}, bf16[16,128]{1,0:T(8,128)(2,1)S(1)}, u32[]{:S(2)}, u32[]{:S(2)}) %collective-permute-start.7) | collective-permute-done | bytes 4128 | tf_op jit(solution)/shard_map/ppermute | solution.py:21
  77.7 2.5 %fusion.6 = bf16[16,2048]{1,0:T(8,128)(2,1)S(1)} fusion(f32[16,2048]{1,0:T(8,128)S(1)} %bitcast_subtract_fusion, bf16[2048,2304]{1,0:T(8,128)(2,1)S(1)} %bitcast.23, bf16[16,128]{1,0:T(8,128)(2,1)S(1)} %collective-permute-done.7, bf16[16,2048]{1,0:T(8,128)(2,1)S(1)} %fusion.5, bf16[16,128]{1,0:T(8,128)(2,1)S(1)} %collective-permute-done.6, ...), kind=kOutput, calls=%fused_computation.13 | convolution fusion | flops 151314432 | bytes 9715712 | tf_op jit(solution)/shard_map/dot_general | solution.py:47
  80.3 1.9 %collective-permute-start.8 = (bf16[16,128]{1,0:T(8,128)(2,1)S(1)}, bf16[16,128]{1,0:T(8,128)(2,1)S(1)}, u32[]{:S(2)}, u32[]{:S(2)}) collective-permute-start(bf16[16,128]{1,0:T(8,128)(2,1)S(1)} %get-tuple-element.4), channel_id=1, source_target_pairs={{0,4},{4,8},{8,12},{12,16},{16,20},{20,24},{24,28},{28,32},{32,36}... | collective-permute-start | bytes 12296 | tf_op jit(solution)/shard_map/ppermute | solution.py:18
  82.2 5.8 %collective-permute-start.9 = (bf16[16,128]{1,0:T(8,128)(2,1)S(1)}, bf16[16,128]{1,0:T(8,128)(2,1)S(1)}, u32[]{:S(2)}, u32[]{:S(2)}) collective-permute-start(bf16[16,128]{1,0:T(8,128)(2,1)S(1)} %get-tuple-element.5), channel_id=1, source_target_pairs={{4,0},{8,4},{12,8},{16,12},{20,16},{24,20},{28,24},{32,28},{36,32}... | collective-permute-start | bytes 12296 | tf_op jit(solution)/shard_map/ppermute | solution.py:21
  88.0 1.3 %collective-permute-done.9 = bf16[16,128]{1,0:T(8,128)(2,1)S(1)} collective-permute-done((bf16[16,128]{1,0:T(8,128)(2,1)S(1)}, bf16[16,128]{1,0:T(8,128)(2,1)S(1)}, u32[]{:S(2)}, u32[]{:S(2)}) %collective-permute-start.9) | collective-permute-done | bytes 4128 | tf_op jit(solution)/shard_map/ppermute | solution.py:21
  89.3 3.2 %constant_dynamic-update-slice_fusion.3 = (bf16[16,8192]{1,0:T(8,128)(2,1)S(1)}, bf16[16,2048]{1,0:T(8,128)(2,1)S(1)}, f32[16,2048]{1,0:T(8,128)}) fusion(bf16[16,8192]{1,0:T(8,128)(2,1)S(1)} %broadcast_in_dim.8, s32[]{:T(128)S(6)} %select_n.36, f32[2048]{0:T(1024)S(1)} %copy-done.1, f32[16,2048]{1,0:T(8,128)S(1)} %bitcast_subtract_fusion, ...), kind=kOutput, calls=%fused_computation.50 | convolution fusion | flops 151314432 | bytes 9912324 | tf_op jit(solution)/shard_map/dot_general | solution.py:47
  92.5 1.6 %collective-permute-start.10 = (bf16[16,2048]{1,0:T(8,128)(2,1)S(1)}, bf16[16,2048]{1,0:T(8,128)(2,1)S(1)}, u32[]{:S(2)}, u32[]{:S(2)}) collective-permute-start(bf16[16,2048]{1,0:T(8,128)(2,1)S(1)} %get-tuple-element.3), channel_id=1, source_target_pairs={{0,1},{1,2},{2,3},{3,0},{4,5},{5,6},{6,7},{7,4},{8,9},{9,10},{10,1... | collective-permute-start | bytes 196616 | tf_op jit(solution)/shard_map/ppermute | solution.py:59
  94.1 1.7 %collective-permute-start.11 = (bf16[16,2048]{1,0:T(8,128)(2,1)S(1)}, bf16[16,2048]{1,0:T(8,128)(2,1)S(1)}, u32[]{:S(2)}, u32[]{:S(2)}) collective-permute-start(bf16[16,2048]{1,0:T(8,128)(2,1)S(1)} %get-tuple-element.3), channel_id=1, source_target_pairs={{0,3},{1,0},{2,1},{3,2},{4,7},{5,4},{6,5},{7,6},{8,11},{9,8},{10,9... | collective-permute-start | bytes 196616 | tf_op jit(solution)/shard_map/ppermute | solution.py:62
  95.8 2.5 %collective-permute-done.10 = bf16[16,2048]{1,0:T(8,128)(2,1)S(1)} collective-permute-done((bf16[16,2048]{1,0:T(8,128)(2,1)S(1)}, bf16[16,2048]{1,0:T(8,128)(2,1)S(1)}, u32[]{:S(2)}, u32[]{:S(2)}) %collective-permute-start.10) | collective-permute-done | bytes 65568 | tf_op jit(solution)/shard_map/ppermute | solution.py:59
  98.3 0.1 collective-permute-start.12
  98.4 5.3 %collective-permute-done.12 = bf16[16,2048]{1,0:T(8,128)(2,1)S(1)} collective-permute-done((bf16[16,2048]{1,0:T(8,128)(2,1)S(1)}, bf16[16,2048]{1,0:T(8,128)(2,1)S(1)}, u32[]{:S(2)}, u32[]{:S(2)}) %collective-permute-start.12) | collective-permute-done | bytes 65568 | tf_op jit(solution)/shard_map/ppermute | solution.py:59
  103.8 0.7 copy-done
  (30 shorter events, 0.2 us)
Async XLA Ops:
  0.6 29.7 %collective-permute-start = (bf16[8,16,8192]{2,1,0:T(8,128)(2,1)}, bf16[8,16,8192]{2,1,0:T(8,128)(2,1)S(1)}, u32[]{:S(2)}, u32[]{:S(2)}) collective-permute-start(bf16[8,16,8192]{2,1,0:T(8,128)(2,1)} %param.12), channel_id=1, source_target_pairs={{0,4},{4,8},{8,12},{12,16},{16,20},{20,24},{24,28},{28,32},{32,36}... | collective-permute-start | bytes 6291464 | tf_op jit(solution)/shard_map/ppermute | solution.py:18
  2.6 29.6 %collective-permute-start.1 = (bf16[8,16,8192]{2,1,0:T(8,128)(2,1)}, bf16[8,16,8192]{2,1,0:T(8,128)(2,1)}, u32[]{:S(2)}, u32[]{:S(2)}) collective-permute-start(bf16[8,16,8192]{2,1,0:T(8,128)(2,1)} %param.12), channel_id=1, source_target_pairs={{4,0},{8,4},{12,8},{16,12},{20,16},{24,20},{28,24},{32,28},{36,32}... | collective-permute-start | bytes 6291464 | tf_op jit(solution)/shard_map/ppermute | solution.py:21
  9.3 41.3 %collective-permute-start.2 = (bf16[16,128]{1,0:T(8,128)(2,1)S(1)}, bf16[16,128]{1,0:T(8,128)(2,1)S(1)}, u32[]{:S(2)}, u32[]{:S(2)}) collective-permute-start(bf16[16,128]{1,0:T(8,128)(2,1)S(1)} %get-tuple-element.10), channel_id=1, source_target_pairs={{0,4},{4,8},{8,12},{12,16},{16,20},{20,24},{24,28},{28,32},{32,36}... | collective-permute-start | bytes 12296 | tf_op jit(solution)/shard_map/ppermute | solution.py:18
  11.3 39.4 %collective-permute-start.3 = (bf16[16,128]{1,0:T(8,128)(2,1)S(1)}, bf16[16,128]{1,0:T(8,128)(2,1)S(1)}, u32[]{:S(2)}, u32[]{:S(2)}) collective-permute-start(bf16[16,128]{1,0:T(8,128)(2,1)S(1)} %get-tuple-element.11), channel_id=1, source_target_pairs={{4,0},{8,4},{12,8},{16,12},{20,16},{24,20},{28,24},{32,28},{36,32}... | collective-permute-start | bytes 12296 | tf_op jit(solution)/shard_map/ppermute | solution.py:21
  41.9 7.0 %copy-start.3 = (s32[256]{0:T(256)S(1)}, s32[256]{0:T(256)}, u32[]{:S(2)}) copy-start(s32[256]{0:T(256)} %param.14) | copy-start | bytes 3076
  41.9 8.7 %copy-start.2 = (f32[16,2048]{1,0:T(8,128)S(1)}, f32[16,2048]{1,0:T(8,128)}, u32[]{:S(2)}) copy-start(f32[16,2048]{1,0:T(8,128)} %param.9) | copy-start | bytes 393220
  41.9 8.8 %copy-start.1 = (f32[2048]{0:T(1024)S(1)}, f32[2048]{0:T(1024)}, u32[]{:S(2)}) copy-start(f32[2048]{0:T(1024)} %param.10) | copy-start | bytes 24580
  41.9 24.3 %slice-start = ((s8[9437184]{0:T(1024)(128)(4,1)}), s8[4194304]{0:T(1024)(128)(4,1)S(1)}, s32[]{:S(2)}) async-start(s8[9437184]{0:T(1024)(128)(4,1)} %bitcast.22), calls=%async_computation | async-start | bytes 8388608
  41.9 24.3 %slice-start.1 = ((s8[9437184]{0:T(1024)(128)(4,1)}), s8[4194304]{0:T(1024)(128)(4,1)S(1)}, s32[]{:S(2)}) async-start(s8[9437184]{0:T(1024)(128)(4,1)} %bitcast.22), calls=%async_computation.1 | async-start | bytes 8388608
  50.7 15.5 %slice-start.2 = ((s8[9437184]{0:T(1024)(128)(4,1)}), s8[1048576]{0:T(1024)(128)(4,1)S(1)}, s32[]{:S(2)}) async-start(s8[9437184]{0:T(1024)(128)(4,1)} %bitcast.22), calls=%async_computation.2 | async-start | bytes 2097152
  57.0 7.9 %collective-permute-start.4 = (bf16[16,128]{1,0:T(8,128)(2,1)S(1)}, bf16[16,128]{1,0:T(8,128)(2,1)S(1)}, u32[]{:S(2)}, u32[]{:S(2)}) collective-permute-start(bf16[16,128]{1,0:T(8,128)(2,1)S(1)} %get-tuple-element.8), channel_id=1, source_target_pairs={{0,4},{4,8},{8,12},{12,16},{16,20},{20,24},{24,28},{28,32},{32,36}... | collective-permute-start | bytes 12296 | tf_op jit(solution)/shard_map/ppermute | solution.py:18
  59.0 7.2 %collective-permute-start.5 = (bf16[16,128]{1,0:T(8,128)(2,1)S(1)}, bf16[16,128]{1,0:T(8,128)(2,1)S(1)}, u32[]{:S(2)}, u32[]{:S(2)}) collective-permute-start(bf16[16,128]{1,0:T(8,128)(2,1)S(1)} %get-tuple-element.9), channel_id=1, source_target_pairs={{4,0},{8,4},{12,8},{16,12},{20,16},{24,20},{28,24},{32,28},{36,32}... | collective-permute-start | bytes 12296 | tf_op jit(solution)/shard_map/ppermute | solution.py:21
  68.7 7.7 %collective-permute-start.6 = (bf16[16,128]{1,0:T(8,128)(2,1)S(1)}, bf16[16,128]{1,0:T(8,128)(2,1)S(1)}, u32[]{:S(2)}, u32[]{:S(2)}) collective-permute-start(bf16[16,128]{1,0:T(8,128)(2,1)S(1)} %get-tuple-element.6), channel_id=1, source_target_pairs={{0,4},{4,8},{8,12},{12,16},{16,20},{20,24},{24,28},{28,32},{32,36}... | collective-permute-start | bytes 12296 | tf_op jit(solution)/shard_map/ppermute | solution.py:18
  70.7 7.1 %collective-permute-start.7 = (bf16[16,128]{1,0:T(8,128)(2,1)S(1)}, bf16[16,128]{1,0:T(8,128)(2,1)S(1)}, u32[]{:S(2)}, u32[]{:S(2)}) collective-permute-start(bf16[16,128]{1,0:T(8,128)(2,1)S(1)} %get-tuple-element.7), channel_id=1, source_target_pairs={{4,0},{8,4},{12,8},{16,12},{20,16},{24,20},{28,24},{32,28},{36,32}... | collective-permute-start | bytes 12296 | tf_op jit(solution)/shard_map/ppermute | solution.py:21
  80.3 7.7 %collective-permute-start.8 = (bf16[16,128]{1,0:T(8,128)(2,1)S(1)}, bf16[16,128]{1,0:T(8,128)(2,1)S(1)}, u32[]{:S(2)}, u32[]{:S(2)}) collective-permute-start(bf16[16,128]{1,0:T(8,128)(2,1)S(1)} %get-tuple-element.4), channel_id=1, source_target_pairs={{0,4},{4,8},{8,12},{12,16},{16,20},{20,24},{24,28},{28,32},{32,36}... | collective-permute-start | bytes 12296 | tf_op jit(solution)/shard_map/ppermute | solution.py:18
  82.2 7.1 %collective-permute-start.9 = (bf16[16,128]{1,0:T(8,128)(2,1)S(1)}, bf16[16,128]{1,0:T(8,128)(2,1)S(1)}, u32[]{:S(2)}, u32[]{:S(2)}) collective-permute-start(bf16[16,128]{1,0:T(8,128)(2,1)S(1)} %get-tuple-element.5), channel_id=1, source_target_pairs={{4,0},{8,4},{12,8},{16,12},{20,16},{24,20},{28,24},{32,28},{36,32}... | collective-permute-start | bytes 12296 | tf_op jit(solution)/shard_map/ppermute | solution.py:21
  92.5 5.8 %collective-permute-start.10 = (bf16[16,2048]{1,0:T(8,128)(2,1)S(1)}, bf16[16,2048]{1,0:T(8,128)(2,1)S(1)}, u32[]{:S(2)}, u32[]{:S(2)}) collective-permute-start(bf16[16,2048]{1,0:T(8,128)(2,1)S(1)} %get-tuple-element.3), channel_id=1, source_target_pairs={{0,1},{1,2},{2,3},{3,0},{4,5},{5,6},{6,7},{7,4},{8,9},{9,10},{10,1... | collective-permute-start | bytes 196616 | tf_op jit(solution)/shard_map/ppermute | solution.py:59
  94.1 4.3 %collective-permute-start.11 = (bf16[16,2048]{1,0:T(8,128)(2,1)S(1)}, bf16[16,2048]{1,0:T(8,128)(2,1)S(1)}, u32[]{:S(2)}, u32[]{:S(2)}) collective-permute-start(bf16[16,2048]{1,0:T(8,128)(2,1)S(1)} %get-tuple-element.3), channel_id=1, source_target_pairs={{0,3},{1,0},{2,1},{3,2},{4,7},{5,4},{6,5},{7,6},{8,11},{9,8},{10,9... | collective-permute-start | bytes 196616 | tf_op jit(solution)/shard_map/ppermute | solution.py:62
  98.3 5.5 %collective-permute-start.12 = (bf16[16,2048]{1,0:T(8,128)(2,1)S(1)}, bf16[16,2048]{1,0:T(8,128)(2,1)S(1)}, u32[]{:S(2)}, u32[]{:S(2)}) collective-permute-start(bf16[16,2048]{1,0:T(8,128)(2,1)S(1)} %collective-permute-done.10), channel_id=1, source_target_pairs={{0,1},{1,2},{2,3},{3,0},{4,5},{5,6},{6,7},{7,4},{8,9},{9,10},{10,1... | collective-permute-start | bytes 196616 | tf_op jit(solution)/shard_map/ppermute | solution.py:59
  103.8 0.7 copy-start
